TPU v7x, 512 devices: a whole 4x8x8 slice. The times are simulated.
512 devices in a mesh: occ: 16 (over y, core), vir: 32 (over x, z).
Axes of the slice: x: 4, y: 8, z: 8, core: 2. Of those that a mesh axis runs over, the one named last changes fastest.
Arguments:
- amplitudes: float32 [2048, 12288], P('occ', 'vir'), may hold values from -6 to 6
- integrals: float32 [12288, 4096], P('vir', 'occ'), may hold values from -0.109375 to 0.109375
- pair_mask: int32 [32, 192], P('occ', 'vir'), may hold values 0 or 1
- tile_mask: int32 [192, 64], P('vir', 'occ'), may hold values 0 or 1
Outputs:
- residual: float32 [2048, 4096], P('occ', 'vir')
Inputs may be any that keep to these rules, and one draw needn't show every extreme that they name: `pair_mask`: 0 marks a tile that is absent and contributes nothing. `tile_mask`: 0 marks a tile that is absent and contributes nothing.
All inputs are finite; a program needn't handle non-finite values. No bound on the sum of `pair_mask` or of `tile_mask` on one device may be relied on, other than what follows from the above.
Results may differ from a plain program's by a relative error of at most 0.00007.
Values sent between devices are 32-bit elements; how exact they have to be, the bound alone decides.
No kernel may reach another device: no remote copies, remote signals or barrier semaphores. Data moves between devices by JAX's collectives and lax.ppermute only.
A program may use at most 64 MiB of HBM per device.

v0:
```python
import jax
import jax.numpy as jnp
from jax import lax
from jax.sharding import Mesh, PartitionSpec as P

AXES = ("h", "l", "c", "x", "z")
SIZES = (4, 2, 2, 4, 8)


def moves(names, target):
    sizes = [SIZES[AXES.index(name)] for name in names]
    pairs = []
    total = 1
    for size in sizes:
        total *= size
    for source in range(total):
        rest, at = (source, {})
        for name, size in zip(names[::-1], sizes[::-1]):
            at[name], rest = (rest % size, rest // size)
        to = dict(at, **target(at))
        index = 0
        for name, size in zip(names, sizes):
            index = index * size + to[name] % size
        pairs.append((source, index))
    return pairs


def send(value, names, target):
    return lax.ppermute(value, names, moves(names, target))


def expand(mask, width):
    grown = jnp.repeat(mask.astype(jnp.float32), width, axis=0)
    return jnp.repeat(grown, width, axis=1)


def product(a, b):
    return jnp.dot(a, b, precision=lax.Precision.HIGH, preferred_element_type=jnp.float32)


def sign(at):
    return 1 - 2 * ((at["x"] + at["c"]) % 2)


def body(amplitudes, integrals, pair_mask, tile_mask):
    l = lax.axis_index("l")
    width = amplitudes.shape[1] // pair_mask.shape[1]
    masked_v = integrals * expand(tile_mask, width)
    far_half = send(masked_v, ("l",), lambda at: {"l": at["l"] + 1})
    near = lax.all_gather(masked_v, "c", axis=1, tiled=True)
    near_beside = send(near, ("c", "x"), lambda at: {"x": at["x"] + sign(at)})
    masked_t = amplitudes * expand(pair_mask, width)
    names = ("h", "c", "x")
    own = jnp.concatenate(
        [
            send(masked_t, names, lambda at: {"h": at["h"] - at["x"]}),
            send(masked_t, names, lambda at: {"h": at["h"] - at["x"] + sign(at)}),
        ]
    )
    beside = jnp.concatenate(
        [
            send(
                masked_t,
                names,
                lambda at: {"h": at["h"] - at["x"] - sign(at), "x": at["x"] + sign(at)},
            ),
            send(
                masked_t,
                names,
                lambda at: {"h": at["h"] - at["x"] - 2 * sign(at), "x": at["x"] + sign(at)},
            ),
        ]
    )
    far = lax.all_gather(far_half, "c", axis=1, tiled=True)
    far_beside = send(far, ("c", "x"), lambda at: {"x": at["x"] + sign(at)})
    near_sum = product(own, near) + product(beside, near_beside)
    far_sum = product(own, far) + product(beside, far_beside)
    away = jnp.concatenate([near_sum[128:], far_sum[128:]], axis=1)
    came = send(away, ("c", "x"), lambda at: {"x": at["x"] - sign(at)})
    near_sum, far_sum = (near_sum[:128] + came[:, :512], far_sum[:128] + came[:, 512:])
    low = l == 0
    halves = jnp.concatenate(
        [jnp.where(low, near_sum, far_sum), jnp.where(low, far_sum, near_sum)], axis=1
    )
    pieces = halves.reshape(128, 8, 128).transpose(1, 0, 2)
    groups = []
    for first in range(0, 512, 8):
        core = first // 32 % 2
        groups.append([first + (k + 4 * core) % 8 for k in range(8)])
    turn = lax.axis_index("c") * 4
    pieces = jnp.concatenate([pieces, pieces[:4]])
    pieces = lax.dynamic_slice_in_dim(pieces, turn, 8, 0)
    total = lax.all_to_all(pieces, AXES, 0, 0, tiled=True, axis_index_groups=groups).sum(0)
    return send(total, ("h", "x"), lambda at: {"h": at["h"] + at["x"], "x": at["h"]})


def solution(mesh):
    fine = Mesh(mesh.devices.reshape(SIZES), AXES)
    occ, vir = (("h", "l", "c"), ("x", "z"))
    in_specs = (P(occ, vir), P(vir, occ), P(occ, vir), P(vir, occ))
    return jax.shard_map(body, mesh=fine, in_specs=in_specs, out_specs=P(occ, vir), check_vma=False)
```

profile of v0, /device:TPU:40, one launch (start us, length us, event | category | flops | bytes accessed | tf_op | source)
XLA Modules:
  0.0 96.9 jit_solution(14063444466938659748)
XLA Ops:
  0.0 0.0 copy-start.4
  0.0 0.0 copy-start.2
  0.0 1.1 %copy.13 = f32[128,384]{0,1:T(8,128)S(1)} copy(f32[128,384]{1,0:T(8,128)} %param.4) | data formatting | bytes 393216 | tf_op args[0]
  1.1 0.0 copy-done.4
  1.1 0.1 copy.12
  1.2 0.1 broadcast_in_dim.12
  1.3 0.1 reshape.15
  1.4 0.0 copy-start.3
  1.4 4.1 %collective-permute-start.2 = (f32[128,384]{0,1:T(8,128)S(1)}, f32[128,384]{0,1:T(8,128)S(1)}, u32[]{:S(2)}, u32[]{:S(2)}) collective-permute-start(f32[128,384]{0,1:T(8,128)S(1)} %bitcast_multiply_fusion.1), channel_id=1, source_target_pairs={{0,392},{8,0},{16,152},{24,272},{32,184},{40,304},{48,424},{56,32}... | collective-permute-start | bytes 589832 | tf_op jit(solution)/shard_map/ppermute | solution.py:29
  5.5 0.0 copy-done.2
  5.5 0.2 copy.14
  5.7 0.0 copy-done.3
  5.7 0.1 broadcast_in_dim.14
  5.8 0.1 reshape.17
  5.9 2.4 %collective-permute-start.5 = (f32[384,256]{0,1:T(8,128)S(1)}, f32[384,256]{0,1:T(8,128)S(1)}, u32[]{:S(2)}, u32[]{:S(2)}) collective-permute-start(f32[384,256]{0,1:T(8,128)S(1)} %bitcast_multiply_fusion), channel_id=1, source_target_pairs={{0,64},{64,0},{1,65},{65,1},{2,66},{66,2},{3,67},{67,3},{4,68},{68... | collective-permute-start | bytes 1179656 | tf_op jit(solution)/shard_map/ppermute | solution.py:29
  8.3 3.0 %all_gather.6 = f32[384,512]{0,1:T(8,128)S(1)} all-gather(f32[384,256]{0,1:T(8,128)S(1)} %bitcast_multiply_fusion), channel_id=1, replica_groups=mesh['h'=4,'l'=2,'c'=2,'x'=4,'z'=8] {'c'}, dimensions={1}, use_global_device_ids=true | all-gather | bytes 1179648 | tf_op jit(solution)/shard_map/all_gather | solution.py:50
  11.2 2.0 %collective-permute-start.4 = (f32[384,512]{0,1:T(8,128)S(1)}, f32[384,512]{0,1:T(8,128)S(1)}, u32[]{:S(2)}, u32[]{:S(2)}) collective-permute-start(f32[384,512]{0,1:T(8,128)S(1)} %all_gather.6), channel_id=1, source_target_pairs={{0,8},{8,0},{16,24},{24,16},{32,56},{40,48},{48,40},{56,32},{1,9},... | collective-permute-start | bytes 2359304 | tf_op jit(solution)/shard_map/ppermute | solution.py:29
  13.3 6.8 %collective-permute-start.3 = (f32[128,384]{0,1:T(8,128)S(1)}, f32[128,384]{0,1:T(8,128)S(1)}, u32[]{:S(2)}, u32[]{:S(2)}) collective-permute-start(f32[128,384]{0,1:T(8,128)S(1)} %bitcast_multiply_fusion.1), channel_id=1, source_target_pairs={{0,264},{8,128},{16,24},{24,400},{32,312},{40,176},{48,40},{56,416... | collective-permute-start | bytes 589832 | tf_op jit(solution)/shard_map/ppermute | solution.py:29
  20.1 0.7 collective-permute-start
  20.8 0.0 collective-permute-done.2
  20.8 4.0 %collective-permute-start.1 = (f32[128,384]{0,1:T(8,128)S(1)}, f32[128,384]{0,1:T(8,128)S(1)}, u32[]{:S(2)}, u32[]{:S(2)}) collective-permute-start(f32[128,384]{0,1:T(8,128)S(1)} %bitcast_multiply_fusion.1), channel_id=1, source_target_pairs={{0,128},{8,264},{16,400},{24,24},{32,416},{40,40},{48,176},{56,312... | collective-permute-start | bytes 589832 | tf_op jit(solution)/shard_map/ppermute | solution.py:29
  24.9 0.0 collective-permute-done.5
  24.9 2.4 %all_gather.7 = f32[384,512]{0,1:T(8,128)S(1)} all-gather(f32[384,256]{0,1:T(8,128)S(1)} %collective-permute-done.5), channel_id=1, replica_groups=mesh['h'=4,'l'=2,'c'=2,'x'=4,'z'=8] {'c'}, dimensions={1}, use_global_device_ids=true | all-gather | bytes 1179648 | tf_op jit(solution)/shard_map/all_gather | solution.py:74
  27.2 7.2 %collective-permute-start.6 = (f32[384,512]{0,1:T(8,128)S(1)}, f32[384,512]{0,1:T(8,128)S(1)}, u32[]{:S(2)}, u32[]{:S(2)}) collective-permute-start(f32[384,512]{0,1:T(8,128)S(1)} %all_gather.7), channel_id=1, source_target_pairs={{0,8},{8,0},{16,24},{24,16},{32,56},{40,48},{48,40},{56,32},{1,9},... | collective-permute-start | bytes 2359304 | tf_op jit(solution)/shard_map/ppermute | solution.py:29
  34.4 0.0 collective-permute-done
  34.5 0.0 collective-permute-done.3
  34.5 1.8 %collective-permute-done.1 = f32[128,384]{0,1:T(8,128)S(1)} collective-permute-done((f32[128,384]{0,1:T(8,128)S(1)}, f32[128,384]{0,1:T(8,128)S(1)}, u32[]{:S(2)}, u32[]{:S(2)}) %collective-permute-start.1) | collective-permute-done | bytes 196640 | tf_op jit(solution)/shard_map/ppermute | solution.py:29
  36.4 0.0 collective-permute-done.4
  36.4 0.9 fusion.1
  37.3 0.9 convolution_add_fusion.1
  38.1 0.0 copy-start
  38.1 0.8 copy-done
  38.9 5.5 %collective-permute-done.6 = f32[384,512]{0,1:T(8,128)S(1)} collective-permute-done((f32[384,512]{0,1:T(8,128)S(1)}, f32[384,512]{0,1:T(8,128)S(1)}, u32[]{:S(2)}, u32[]{:S(2)}) %collective-permute-start.6) | collective-permute-done | bytes 786464 | tf_op jit(solution)/shard_map/ppermute | solution.py:29
  44.4 0.9 fusion.2
  45.3 0.9 convolution_add_fusion
  46.1 0.0 slice-start
  46.2 0.9 slice-done
  47.1 0.0 copy-start.1
  47.1 4.1 %collective-permute-start.7 = (f32[128,1024]{1,0:T(8,128)S(1)}, f32[128,1024]{1,0:T(8,128)S(1)}, u32[]{:S(2)}, u32[]{:S(2)}) collective-permute-start(f32[128,1024]{1,0:T(8,128)S(1)} %pad_maximum_fusion), channel_id=1, source_target_pairs={{0,24},{8,16},{16,8},{24,0},{32,40},{40,32},{48,56},{56,48},{1,25}... | collective-permute-start | bytes 1572872 | tf_op jit(solution)/shard_map/ppermute | solution.py:29
  51.3 8.3 %collective-permute-done.7 = f32[128,1024]{1,0:T(8,128)S(1)} collective-permute-done((f32[128,1024]{1,0:T(8,128)S(1)}, f32[128,1024]{1,0:T(8,128)S(1)}, u32[]{:S(2)}, u32[]{:S(2)}) %collective-permute-start.7) | collective-permute-done | bytes 524320 | tf_op jit(solution)/shard_map/ppermute | solution.py:29
  59.6 0.0 copy-done.1
  59.6 0.1 broadcast_select_fusion.1
  59.7 0.1 fusion
  59.8 23.2 %all_to_all.5 = f32[8,128,128]{2,1,0:T(8,128)S(1)} all-to-all(f32[8,128,128]{2,1,0:T(8,128)S(1)} %fusion), channel_id=1, replica_groups={{0,1,2,3,4,5,6,7},{8,9,10,11,12,13,14,15},{16,17,18,19,20,21,22,23},{24..., dimensions={0} | all-to-all | bytes 1048576 | tf_op jit(solution)/shard_map/all_to_all | solution.py:93
  83.0 4.6 %collective-permute-start.8 = (f32[128,128]{1,0:T(8,128)S(1)}, f32[128,128]{1,0:T(8,128)S(1)}, u32[]{:S(2)}, u32[]{:S(2)}) collective-permute-start(f32[128,128]{1,0:T(8,128)S(1)} %reduce_sum.9), channel_id=1, source_target_pairs={{0,0},{8,128},{16,256},{24,384},{128,136},{136,264},{144,392},{152... | collective-permute-start | bytes 196616 | tf_op jit(solution)/shard_map/ppermute | solution.py:29
  87.6 8.6 %collective-permute-done.8 = f32[128,128]{1,0:T(8,128)S(1)} collective-permute-done((f32[128,128]{1,0:T(8,128)S(1)}, f32[128,128]{1,0:T(8,128)S(1)}, u32[]{:S(2)}, u32[]{:S(2)}) %collective-permute-start.8) | collective-permute-done | bytes 65568 | tf_op jit(solution)/shard_map/ppermute | solution.py:29
  96.2 0.6 copy.21
  (13 shorter events, 0.3 us)
Async XLA Ops:
  0.0 1.1 %copy-start.4 = (s32[2,6]{1,0:T(2,128)S(1)}, s32[2,6]{1,0:T(2,128)}, u32[]{:S(2)}) copy-start(s32[2,6]{1,0:T(2,128)} %param.6) | copy-start | bytes 148
  0.0 5.5 %copy-start.2 = (f32[384,256]{1,0:T(8,128)S(1)}, f32[384,256]{1,0:T(8,128)}, u32[]{:S(2)}) copy-start(f32[384,256]{1,0:T(8,128)} %param.5) | copy-start | bytes 1179652
  1.4 4.3 %copy-start.3 = (s32[6,4]{0,1:T(4,128)S(1)}, s32[6,4]{0,1:T(4,128)}, u32[]{:S(2)}) copy-start(s32[6,4]{0,1:T(4,128)} %param.7) | copy-start | bytes 292
  1.4 19.4 %collective-permute-start.2 = (f32[128,384]{0,1:T(8,128)S(1)}, f32[128,384]{0,1:T(8,128)S(1)}, u32[]{:S(2)}, u32[]{:S(2)}) collective-permute-start(f32[128,384]{0,1:T(8,128)S(1)} %bitcast_multiply_fusion.1), channel_id=1, source_target_pairs={{0,392},{8,0},{16,152},{24,272},{32,184},{40,304},{48,424},{56,32}... | collective-permute-start | bytes 589832 | tf_op jit(solution)/shard_map/ppermute | solution.py:29
  5.9 19.0 %collective-permute-start.5 = (f32[384,256]{0,1:T(8,128)S(1)}, f32[384,256]{0,1:T(8,128)S(1)}, u32[]{:S(2)}, u32[]{:S(2)}) collective-permute-start(f32[384,256]{0,1:T(8,128)S(1)} %bitcast_multiply_fusion), channel_id=1, source_target_pairs={{0,64},{64,0},{1,65},{65,1},{2,66},{66,2},{3,67},{67,3},{4,68},{68... | collective-permute-start | bytes 1179656 | tf_op jit(solution)/shard_map/ppermute | solution.py:29
  11.2 25.1 %collective-permute-start.4 = (f32[384,512]{0,1:T(8,128)S(1)}, f32[384,512]{0,1:T(8,128)S(1)}, u32[]{:S(2)}, u32[]{:S(2)}) collective-permute-start(f32[384,512]{0,1:T(8,128)S(1)} %all_gather.6), channel_id=1, source_target_pairs={{0,8},{8,0},{16,24},{24,16},{32,56},{40,48},{48,40},{56,32},{1,9},... | collective-permute-start | bytes 2359304 | tf_op jit(solution)/shard_map/ppermute | solution.py:29
  13.3 21.2 %collective-permute-start.3 = (f32[128,384]{0,1:T(8,128)S(1)}, f32[128,384]{0,1:T(8,128)S(1)}, u32[]{:S(2)}, u32[]{:S(2)}) collective-permute-start(f32[128,384]{0,1:T(8,128)S(1)} %bitcast_multiply_fusion.1), channel_id=1, source_target_pairs={{0,264},{8,128},{16,24},{24,400},{32,312},{40,176},{48,40},{56,416... | collective-permute-start | bytes 589832 | tf_op jit(solution)/shard_map/ppermute | solution.py:29
  20.1 14.3 %collective-permute-start = (f32[128,384]{0,1:T(8,128)S(1)}, f32[128,384]{0,1:T(8,128)S(1)}, u32[]{:S(2)}, u32[]{:S(2)}) collective-permute-start(f32[128,384]{0,1:T(8,128)S(1)} %bitcast_multiply_fusion.1), channel_id=1, source_target_pairs={{0,0},{8,392},{16,272},{24,152},{32,32},{40,424},{48,304},{56,184}... | collective-permute-start | bytes 589832 | tf_op jit(solution)/shard_map/ppermute | solution.py:29
  20.8 15.5 %collective-permute-start.1 = (f32[128,384]{0,1:T(8,128)S(1)}, f32[128,384]{0,1:T(8,128)S(1)}, u32[]{:S(2)}, u32[]{:S(2)}) collective-permute-start(f32[128,384]{0,1:T(8,128)S(1)} %bitcast_multiply_fusion.1), channel_id=1, source_target_pairs={{0,128},{8,264},{16,400},{24,24},{32,416},{40,40},{48,176},{56,312... | collective-permute-start | bytes 589832 | tf_op jit(solution)/shard_map/ppermute | solution.py:29
  27.2 17.1 %collective-permute-start.6 = (f32[384,512]{0,1:T(8,128)S(1)}, f32[384,512]{0,1:T(8,128)S(1)}, u32[]{:S(2)}, u32[]{:S(2)}) collective-permute-start(f32[384,512]{0,1:T(8,128)S(1)} %all_gather.7), channel_id=1, source_target_pairs={{0,8},{8,0},{16,24},{24,16},{32,56},{40,48},{48,40},{56,32},{1,9},... | collective-permute-start | bytes 2359304 | tf_op jit(solution)/shard_map/ppermute | solution.py:29
  38.1 0.8 copy-start
  46.1 1.0 slice-start
  47.1 12.5 %copy-start.1 = (f32[256,512]{1,0:T(8,128)S(1)}, f32[256,512]{1,0:T(8,128)}, u32[]{:S(2)}) copy-start(f32[256,512]{1,0:T(8,128)} %copy-done) | copy-start | bytes 1572868
  47.1 12.4 %collective-permute-start.7 = (f32[128,1024]{1,0:T(8,128)S(1)}, f32[128,1024]{1,0:T(8,128)S(1)}, u32[]{:S(2)}, u32[]{:S(2)}) collective-permute-start(f32[128,1024]{1,0:T(8,128)S(1)} %pad_maximum_fusion), channel_id=1, source_target_pairs={{0,24},{8,16},{16,8},{24,0},{32,40},{40,32},{48,56},{56,48},{1,25}... | collective-permute-start | bytes 1572872 | tf_op jit(solution)/shard_map/ppermute | solution.py:29
  83.0 13.2 %collective-permute-start.8 = (f32[128,128]{1,0:T(8,128)S(1)}, f32[128,128]{1,0:T(8,128)S(1)}, u32[]{:S(2)}, u32[]{:S(2)}) collective-permute-start(f32[128,128]{1,0:T(8,128)S(1)} %reduce_sum.9), channel_id=1, source_target_pairs={{0,0},{8,128},{16,256},{24,384},{128,136},{136,264},{144,392},{152... | collective-permute-start | bytes 196616 | tf_op jit(solution)/shard_map/ppermute | solution.py:29
where the time goes:
time: 97.3 us; the launch traced here: 96.9 us
  starting transfers between devices  35.9 us (37%)
  blocking collectives  28.6 us (29%)
  waiting for transfers between devices  24.2 us (25%)
  local copies, waits for them, and re-layouts  4.11 us (4%)
  matrix products  3.49 us (4%)
    ppermute x9, starting transfers between devices, send(): return lax.ppermute(value, names, moves(names, target))  35.9 us
    ppermute x9, waiting for transfers between devices, send(): return lax.ppermute(value, names, moves(names, target))  24.2 us
    all_to_all x1, blocking collectives, body(): lax.all_to_all(pieces, AXES, 0, 0, tiled=True, axis_index_groups=groups)  23.2 us
    dot_general x4, matrix products, product(): jnp.dot(a, b, precision=lax.Precision.HIGH, preferred_element_type=jnp.fl...  3.49 us
    all_gather x1, blocking collectives, body(): near = lax.all_gather(masked_v, 'c', axis=1, tiled=True)  2.99 us
    unnamed x15, local copies, waits for them, and re-layouts  2.73 us
    all_gather x1, blocking collectives, body(): far = lax.all_gather(far_half, 'c', axis=1, tiled=True)  2.37 us
  transfers between devices with their start and end apart: 9, of which 4 were waited for; matrix products, arithmetic and copies ran while one was open for 2% of the time, Pallas kernels for 0%

commit v1 on v0

--- a/solution.py
+++ b/solution.py
@@ -47,7 +47,9 @@
     width = amplitudes.shape[1] // pair_mask.shape[1]
     masked_v = integrals * expand(tile_mask, width)
     far_half = send(masked_v, ("l",), lambda at: {"l": at["l"] + 1})
-    near = lax.all_gather(masked_v, "c", axis=1, tiled=True)
+    near = jnp.concatenate(
+        lax.all_to_all(jnp.stack([masked_v] * lax.axis_size("c")), "c", 0, 0), axis=1
+    )
     near_beside = send(near, ("c", "x"), lambda at: {"x": at["x"] + sign(at)})
     masked_t = amplitudes * expand(pair_mask, width)
     names = ("h", "c", "x")

time: 97.3 us -> 99.5 us (1.023)
  blocking collectives: 28.6 us -> 30.5 us
    all_to_all x0 -> x1, blocking collectives: none -> 4.86 us  [body(): lax.all_to_all(jnp.stack([masked_v] * lax.axis_size('c')), 'c', 0, 0)]
    all_gather x1 -> x0, blocking collectives: 2.99 us -> none  [body(): near = lax.all_gather(masked_v, 'c', axis=1, tiled=True)]
where the time goes in v1:
time: 99.5 us; the launch traced here: 99.1 us
  starting transfers between devices  36.1 us (36%)
  blocking collectives  30.5 us (31%)
  waiting for transfers between devices  24.1 us (24%)
  local copies, waits for them, and re-layouts  4.14 us (4%)
  matrix products  3.48 us (3%)
    ppermute x9, starting transfers between devices, send(): return lax.ppermute(value, names, moves(names, target))  36.1 us
    ppermute x9, waiting for transfers between devices, send(): return lax.ppermute(value, names, moves(names, target))  24.1 us
    all_to_all x1, blocking collectives, body(): lax.all_to_all(pieces, AXES, 0, 0, tiled=True, axis_index_groups=groups)  23.2 us
    all_to_all x1, blocking collectives, body(): lax.all_to_all(jnp.stack([masked_v] * lax.axis_size('c')), 'c', 0, 0)  4.86 us
    dot_general x4, matrix products, product(): jnp.dot(a, b, precision=lax.Precision.HIGH, preferred_element_type=jnp.fl...  3.48 us
    unnamed x15, local copies, waits for them, and re-layouts  2.75 us
    all_gather x1, blocking collectives, body(): far = lax.all_gather(far_half, 'c', axis=1, tiled=True)  2.46 us
  transfers between devices with their start and end apart: 9, of which 4 were waited for; matrix products, arithmetic and copies ran while one was open for 2% of the time, Pallas kernels for 0%

profile of v1, /device:TPU:40, one launch (start us, length us, event | category | flops | bytes accessed | tf_op | source)
XLA Modules:
  0.0 99.1 jit_solution(8597249875948697194)
XLA Ops:
  0.0 0.0 copy-start.3
  0.0 1.2 %copy.14 = f32[384,256]{0,1:T(8,128)S(1)} copy(f32[384,256]{1,0:T(8,128)} %param.5) | data formatting | bytes 786432 | tf_op args[1]
  1.2 0.0 copy-done.3
  1.2 0.1 broadcast_in_dim.14
  1.3 0.1 reshape.23
  1.4 0.0 copy-start.2
  1.4 0.0 copy-start.4
  1.4 3.4 %collective-permute-start.5 = (f32[384,256]{0,1:T(8,128)S(1)}, f32[384,256]{0,1:T(8,128)S(1)}, u32[]{:S(2)}, u32[]{:S(2)}) collective-permute-start(f32[384,256]{0,1:T(8,128)S(1)} %bitcast_multiply_fusion), channel_id=1, source_target_pairs={{0,64},{64,0},{1,65},{65,1},{2,66},{66,2},{3,67},{67,3},{4,68},{68... | collective-permute-start | bytes 1179656 | tf_op jit(solution)/shard_map/ppermute | solution.py:29
  4.8 0.0 copy-done.2
  4.8 0.1 copy.13
  4.9 0.0 copy-done.4
  5.0 0.1 copy.12
  5.1 0.1 broadcast_in_dim.12
  5.1 0.1 reshape.21
  5.2 3.2 %collective-permute-start.2 = (f32[128,384]{0,1:T(8,128)S(1)}, f32[128,384]{0,1:T(8,128)S(1)}, u32[]{:S(2)}, u32[]{:S(2)}) collective-permute-start(f32[128,384]{0,1:T(8,128)S(1)} %bitcast_multiply_fusion.1), channel_id=1, source_target_pairs={{0,392},{8,0},{16,152},{24,272},{32,184},{40,304},{48,424},{56,32}... | collective-permute-start | bytes 589832 | tf_op jit(solution)/shard_map/ppermute | solution.py:29
  8.4 0.1 pad_maximum_fusion
  8.5 4.9 %all_to_all.10 = f32[2,384,256]{1,2,0:T(8,128)S(1)} all-to-all(f32[2,384,256]{1,2,0:T(8,128)S(1)} %pad_maximum_fusion), channel_id=1, replica_groups=mesh['h'=4,'l'=2,'c'=2,'x'=4,'z'=8] {'c'}, dimensions={0} | all-to-all | bytes 1572864 | tf_op jit(solution)/shard_map/all_to_all | solution.py:51
  13.3 2.2 %collective-permute-start.4 = (f32[384,512]{0,1:T(8,128)S(1)}, f32[384,512]{0,1:T(8,128)S(1)}, u32[]{:S(2)}, u32[]{:S(2)}) collective-permute-start(f32[384,512]{0,1:T(8,128)S(1)} %bitcast.27), channel_id=1, source_target_pairs={{0,8},{8,0},{16,24},{24,16},{32,56},{40,48},{48,40},{56,32},{1,9},... | collective-permute-start | bytes 2359304 | tf_op jit(solution)/shard_map/ppermute | solution.py:29
  15.5 6.8 %collective-permute-start.3 = (f32[128,384]{0,1:T(8,128)S(1)}, f32[128,384]{0,1:T(8,128)S(1)}, u32[]{:S(2)}, u32[]{:S(2)}) collective-permute-start(f32[128,384]{0,1:T(8,128)S(1)} %bitcast_multiply_fusion.1), channel_id=1, source_target_pairs={{0,264},{8,128},{16,24},{24,400},{32,312},{40,176},{48,40},{56,416... | collective-permute-start | bytes 589832 | tf_op jit(solution)/shard_map/ppermute | solution.py:29
  22.4 0.7 collective-permute-start
  23.0 0.0 collective-permute-done.2
  23.0 3.9 %collective-permute-start.1 = (f32[128,384]{0,1:T(8,128)S(1)}, f32[128,384]{0,1:T(8,128)S(1)}, u32[]{:S(2)}, u32[]{:S(2)}) collective-permute-start(f32[128,384]{0,1:T(8,128)S(1)} %bitcast_multiply_fusion.1), channel_id=1, source_target_pairs={{0,128},{8,264},{16,400},{24,24},{32,416},{40,40},{48,176},{56,312... | collective-permute-start | bytes 589832 | tf_op jit(solution)/shard_map/ppermute | solution.py:29
  27.0 0.0 collective-permute-done.5
  27.0 2.5 %all_gather.3 = f32[384,512]{0,1:T(8,128)S(1)} all-gather(f32[384,256]{0,1:T(8,128)S(1)} %collective-permute-done.5), channel_id=1, replica_groups=mesh['h'=4,'l'=2,'c'=2,'x'=4,'z'=8] {'c'}, dimensions={1}, use_global_device_ids=true | all-gather | bytes 1179648 | tf_op jit(solution)/shard_map/all_gather | solution.py:76
  29.4 7.2 %collective-permute-start.6 = (f32[384,512]{0,1:T(8,128)S(1)}, f32[384,512]{0,1:T(8,128)S(1)}, u32[]{:S(2)}, u32[]{:S(2)}) collective-permute-start(f32[384,512]{0,1:T(8,128)S(1)} %all_gather.3), channel_id=1, source_target_pairs={{0,8},{8,0},{16,24},{24,16},{32,56},{40,48},{48,40},{56,32},{1,9},... | collective-permute-start | bytes 2359304 | tf_op jit(solution)/shard_map/ppermute | solution.py:29
  36.7 0.0 collective-permute-done
  36.7 0.0 collective-permute-done.3
  36.7 1.8 %collective-permute-done.1 = f32[128,384]{0,1:T(8,128)S(1)} collective-permute-done((f32[128,384]{0,1:T(8,128)S(1)}, f32[128,384]{0,1:T(8,128)S(1)}, u32[]{:S(2)}, u32[]{:S(2)}) %collective-permute-start.1) | collective-permute-done | bytes 196640 | tf_op jit(solution)/shard_map/ppermute | solution.py:29
  38.6 0.0 collective-permute-done.4
  38.6 0.9 fusion.1
  39.5 0.9 convolution_add_fusion.1
  40.4 0.0 copy-start
  40.4 0.8 copy-done
  41.1 5.5 %collective-permute-done.6 = f32[384,512]{0,1:T(8,128)S(1)} collective-permute-done((f32[384,512]{0,1:T(8,128)S(1)}, f32[384,512]{0,1:T(8,128)S(1)}, u32[]{:S(2)}, u32[]{:S(2)}) %collective-permute-start.6) | collective-permute-done | bytes 786464 | tf_op jit(solution)/shard_map/ppermute | solution.py:29
  46.6 0.9 fusion.2
  47.5 0.9 convolution_add_fusion
  48.4 0.0 slice-start
  48.4 0.9 slice-done
  49.3 0.0 copy-start.1
  49.3 4.2 %collective-permute-start.7 = (f32[128,1024]{1,0:T(8,128)S(1)}, f32[128,1024]{1,0:T(8,128)S(1)}, u32[]{:S(2)}, u32[]{:S(2)}) collective-permute-start(f32[128,1024]{1,0:T(8,128)S(1)} %pad_maximum_fusion.1), channel_id=1, source_target_pairs={{0,24},{8,16},{16,8},{24,0},{32,40},{40,32},{48,56},{56,48},{1,25}... | collective-permute-start | bytes 1572872 | tf_op jit(solution)/shard_map/ppermute | solution.py:29
  53.5 8.3 %collective-permute-done.7 = f32[128,1024]{1,0:T(8,128)S(1)} collective-permute-done((f32[128,1024]{1,0:T(8,128)S(1)}, f32[128,1024]{1,0:T(8,128)S(1)}, u32[]{:S(2)}, u32[]{:S(2)}) %collective-permute-start.7) | collective-permute-done | bytes 524320 | tf_op jit(solution)/shard_map/ppermute | solution.py:29
  61.8 0.0 copy-done.1
  61.8 0.1 broadcast_select_fusion.1
  61.9 0.1 fusion
  62.0 23.2 %all_to_all.11 = f32[8,128,128]{2,1,0:T(8,128)S(1)} all-to-all(f32[8,128,128]{2,1,0:T(8,128)S(1)} %fusion), channel_id=1, replica_groups={{0,1,2,3,4,5,6,7},{8,9,10,11,12,13,14,15},{16,17,18,19,20,21,22,23},{24..., dimensions={0} | all-to-all | bytes 1048576 | tf_op jit(solution)/shard_map/all_to_all | solution.py:95
  85.3 4.6 %collective-permute-start.8 = (f32[128,128]{1,0:T(8,128)S(1)}, f32[128,128]{1,0:T(8,128)S(1)}, u32[]{:S(2)}, u32[]{:S(2)}) collective-permute-start(f32[128,128]{1,0:T(8,128)S(1)} %reduce_sum.9), channel_id=1, source_target_pairs={{0,0},{8,128},{16,256},{24,384},{128,136},{136,264},{144,392},{152... | collective-permute-start | bytes 196616 | tf_op jit(solution)/shard_map/ppermute | solution.py:29
  89.9 8.6 %collective-permute-done.8 = f32[128,128]{1,0:T(8,128)S(1)} collective-permute-done((f32[128,128]{1,0:T(8,128)S(1)}, f32[128,128]{1,0:T(8,128)S(1)}, u32[]{:S(2)}, u32[]{:S(2)}) %collective-permute-start.8) | collective-permute-done | bytes 65568 | tf_op jit(solution)/shard_map/ppermute | solution.py:29
  98.4 0.6 copy.21
  (13 shorter events, 0.3 us)
Async XLA Ops:
  0.0 1.2 %copy-start.3 = (s32[6,4]{0,1:T(4,128)S(1)}, s32[6,4]{0,1:T(4,128)}, u32[]{:S(2)}) copy-start(s32[6,4]{0,1:T(4,128)} %param.7) | copy-start | bytes 292
  1.4 3.4 %copy-start.2 = (f32[128,384]{1,0:T(8,128)S(1)}, f32[128,384]{1,0:T(8,128)}, u32[]{:S(2)}) copy-start(f32[128,384]{1,0:T(8,128)} %param.4) | copy-start | bytes 589828
  1.4 3.5 %copy-start.4 = (s32[2,6]{1,0:T(2,128)S(1)}, s32[2,6]{1,0:T(2,128)}, u32[]{:S(2)}) copy-start(s32[2,6]{1,0:T(2,128)} %param.6) | copy-start | bytes 148
  1.4 25.6 %collective-permute-start.5 = (f32[384,256]{0,1:T(8,128)S(1)}, f32[384,256]{0,1:T(8,128)S(1)}, u32[]{:S(2)}, u32[]{:S(2)}) collective-permute-start(f32[384,256]{0,1:T(8,128)S(1)} %bitcast_multiply_fusion), channel_id=1, source_target_pairs={{0,64},{64,0},{1,65},{65,1},{2,66},{66,2},{3,67},{67,3},{4,68},{68... | collective-permute-start | bytes 1179656 | tf_op jit(solution)/shard_map/ppermute | solution.py:29
  5.2 17.8 %collective-permute-start.2 = (f32[128,384]{0,1:T(8,128)S(1)}, f32[128,384]{0,1:T(8,128)S(1)}, u32[]{:S(2)}, u32[]{:S(2)}) collective-permute-start(f32[128,384]{0,1:T(8,128)S(1)} %bitcast_multiply_fusion.1), channel_id=1, source_target_pairs={{0,392},{8,0},{16,152},{24,272},{32,184},{40,304},{48,424},{56,32}... | collective-permute-start | bytes 589832 | tf_op jit(solution)/shard_map/ppermute | solution.py:29
  13.3 25.2 %collective-permute-start.4 = (f32[384,512]{0,1:T(8,128)S(1)}, f32[384,512]{0,1:T(8,128)S(1)}, u32[]{:S(2)}, u32[]{:S(2)}) collective-permute-start(f32[384,512]{0,1:T(8,128)S(1)} %bitcast.27), channel_id=1, source_target_pairs={{0,8},{8,0},{16,24},{24,16},{32,56},{40,48},{48,40},{56,32},{1,9},... | collective-permute-start | bytes 2359304 | tf_op jit(solution)/shard_map/ppermute | solution.py:29
  15.5 21.2 %collective-permute-start.3 = (f32[128,384]{0,1:T(8,128)S(1)}, f32[128,384]{0,1:T(8,128)S(1)}, u32[]{:S(2)}, u32[]{:S(2)}) collective-permute-start(f32[128,384]{0,1:T(8,128)S(1)} %bitcast_multiply_fusion.1), channel_id=1, source_target_pairs={{0,264},{8,128},{16,24},{24,400},{32,312},{40,176},{48,40},{56,416... | collective-permute-start | bytes 589832 | tf_op jit(solution)/shard_map/ppermute | solution.py:29
  22.4 14.3 %collective-permute-start = (f32[128,384]{0,1:T(8,128)S(1)}, f32[128,384]{0,1:T(8,128)S(1)}, u32[]{:S(2)}, u32[]{:S(2)}) collective-permute-start(f32[128,384]{0,1:T(8,128)S(1)} %bitcast_multiply_fusion.1), channel_id=1, source_target_pairs={{0,0},{8,392},{16,272},{24,152},{32,32},{40,424},{48,304},{56,184}... | collective-permute-start | bytes 589832 | tf_op jit(solution)/shard_map/ppermute | solution.py:29
  23.0 15.5 %collective-permute-start.1 = (f32[128,384]{0,1:T(8,128)S(1)}, f32[128,384]{0,1:T(8,128)S(1)}, u32[]{:S(2)}, u32[]{:S(2)}) collective-permute-start(f32[128,384]{0,1:T(8,128)S(1)} %bitcast_multiply_fusion.1), channel_id=1, source_target_pairs={{0,128},{8,264},{16,400},{24,24},{32,416},{40,40},{48,176},{56,312... | collective-permute-start | bytes 589832 | tf_op jit(solution)/shard_map/ppermute | solution.py:29
  29.4 17.2 %collective-permute-start.6 = (f32[384,512]{0,1:T(8,128)S(1)}, f32[384,512]{0,1:T(8,128)S(1)}, u32[]{:S(2)}, u32[]{:S(2)}) collective-permute-start(f32[384,512]{0,1:T(8,128)S(1)} %all_gather.3), channel_id=1, source_target_pairs={{0,8},{8,0},{16,24},{24,16},{32,56},{40,48},{48,40},{56,32},{1,9},... | collective-permute-start | bytes 2359304 | tf_op jit(solution)/shard_map/ppermute | solution.py:29
  40.4 0.8 copy-start
  48.4 1.0 slice-start
  49.3 12.5 %copy-start.1 = (f32[256,512]{1,0:T(8,128)S(1)}, f32[256,512]{1,0:T(8,128)}, u32[]{:S(2)}) copy-start(f32[256,512]{1,0:T(8,128)} %copy-done) | copy-start | bytes 1572868
  49.3 12.4 %collective-permute-start.7 = (f32[128,1024]{1,0:T(8,128)S(1)}, f32[128,1024]{1,0:T(8,128)S(1)}, u32[]{:S(2)}, u32[]{:S(2)}) collective-permute-start(f32[128,1024]{1,0:T(8,128)S(1)} %pad_maximum_fusion.1), channel_id=1, source_target_pairs={{0,24},{8,16},{16,8},{24,0},{32,40},{40,32},{48,56},{56,48},{1,25}... | collective-permute-start | bytes 1572872 | tf_op jit(solution)/shard_map/ppermute | solution.py:29
  85.3 13.2 %collective-permute-start.8 = (f32[128,128]{1,0:T(8,128)S(1)}, f32[128,128]{1,0:T(8,128)S(1)}, u32[]{:S(2)}, u32[]{:S(2)}) collective-permute-start(f32[128,128]{1,0:T(8,128)S(1)} %reduce_sum.9), channel_id=1, source_target_pairs={{0,0},{8,128},{16,256},{24,384},{128,136},{136,264},{144,392},{152... | collective-permute-start | bytes 196616 | tf_op jit(solution)/shard_map/ppermute | solution.py:29
